TPU v7x, 32 devices: a whole 2x2x4 slice. The times are simulated.
32 devices in a mesh: dp: 4 (over x, core), expert: 8 (over z, y).
Axes of the slice: x: 2, y: 2, z: 4, core: 2. Of those that a mesh axis runs over, the one named last changes fastest.
Arguments:
- tokens_in: bfloat16 [2, 256, 2048], P(None, 'expert', 'dp'), may hold values from -6 to 6
- route_ids: int32 [2, 256, 8], P(None, 'expert'), may hold values from 0 to 15, all different within a row; in each aligned block of 32 rows (0 to 31, 32 to 63, ..., all dimensions but the last counted through in order) at most 32 rows name the same one
- route_gates: float32 [2, 256, 8], P(None, 'expert'), may hold values from 0.1 to 1
- cotangent: bfloat16 [2, 256, 2048], P(None, 'expert', 'dp'), may hold values from -0.75 to 0.75
- gate_proj: bfloat16 [16, 1024, 1536], P(None, 'expert', 'dp'), may hold values from -0.125 to 0.125
- up_proj: bfloat16 [16, 1024, 1536], P(None, 'expert', 'dp'), may hold values from -0.125 to 0.125
- down_proj: bfloat16 [16, 1024, 1536], P(None, 'expert', 'dp'), may hold values from -0.21875 to 0.21875
- replica_plan: int32 [2, 8], replicated, may hold values from 0 to 15, as said below
- capacity: int32 [2, 16], replicated, may hold values from 8 to 16, as said below
Outputs:
- y_out: bfloat16 [2, 256, 2048], P(None, 'expert', 'dp')
- x_grad: bfloat16 [2, 256, 2048], P(None, 'expert', 'dp')
- gate_grad: bfloat16 [16, 1024, 1536], P(None, 'expert', 'dp')
- up_grad: bfloat16 [16, 1024, 1536], P(None, 'expert', 'dp')
- down_grad: bfloat16 [16, 1024, 1536], P(None, 'expert', 'dp')
Inputs may be any that keep to these rules, and one draw needn't show every extreme that they name: `route_ids`: each token names 8 different experts; among the tokens of one micro-batch on one index of the expert axis (an aligned block of 32), no expert is named more than 2 * 16 times. `replica_plan`: an expert may fill the replica slot of several devices, or of none. Some expert has capacity 16 in every micro-batch.
All inputs are finite; a program needn't handle non-finite values.
Results may differ from a plain program's by a relative error of at most 0.012.
Values may be sent and summed in bfloat16 or wider, within the bound.
A program may use at most 192 MiB of HBM per device.

v0:
```python
import functools

import jax
import jax.numpy as jnp
from jax import lax
from jax.experimental import pallas as pl
from jax.experimental.pallas import tpu as pltpu
from jax.sharding import PartitionSpec as P

GROUP = 16
BF = jnp.bfloat16
F32 = jnp.float32


def kept_routes(batch_ids, batch_plan, batch_caps, source, device_count):
    expert_count = batch_caps.shape[0]
    tok_count = batch_ids.shape[0]
    expert_ids = jnp.arange(expert_count, dtype=jnp.int32)
    hosting = (batch_plan[None, :] == expert_ids[:, None]).astype(jnp.int32)
    ranking = jnp.cumsum(hosting, axis=1)
    copies = 1 + ranking[:, -1]
    matches = (batch_ids[:, :, None] == expert_ids[None, None, :]).astype(jnp.int32)
    copies_route = jnp.sum(matches * copies[None, None, :], axis=2)
    limits = jnp.sum(matches * batch_caps[None, None, :], axis=2)
    token_ids = source * tok_count + jnp.arange(tok_count, dtype=jnp.int32)
    chosen = token_ids[:, None] % copies_route
    flat = (batch_ids * (device_count + 1) + chosen).reshape(-1)
    place = jnp.arange(flat.shape[0], dtype=jnp.int32)
    earlier = (flat[:, None] == flat[None, :]) & (place[None, :] < place[:, None])
    before = jnp.sum(earlier.astype(jnp.int32), axis=1).reshape(batch_ids.shape)
    return before < limits


def pairing(features, inverse):
    half = features // 2
    a = lax.broadcasted_iota(jnp.int32, (features, features), 0)
    b = lax.broadcasted_iota(jnp.int32, (features, features), 1)
    if inverse:
        a, b = b, a
    return (a == 2 * (b % half) + b // half).astype(F32).astype(BF)


def dot(a, b, dims=((1,), (0,))):
    return lax.dot_general(a, b, (dims, ((), ())), preferred_element_type=F32)


def stacked(w):
    half = w.shape[1] // 2
    return jnp.concatenate([w[:, :half], w[:, half:]], axis=0)


def pre_kernel(xc_ref, want_ref, wg_ref, wu_ref, wd_ref, out_ref, p_ref):
    experts = wg_ref.shape[0]
    features = 2 * wg_ref.shape[1]
    hidden = wg_ref.shape[2] // 2
    tokens = xc_ref.shape[0]
    top = want_ref.shape[0] // tokens
    perm = pairing(features, False)
    x = dot(xc_ref[:, :features], perm).astype(BF)
    c = dot(xc_ref[:, features:], perm).astype(BF)

    def expert(e, carry):
        for kind, (w_ref, rows) in enumerate(((wg_ref, x), (wu_ref, x), (wd_ref, c))):
            p_ref[kind, e] = dot(rows, stacked(w_ref[e])).astype(BF)
        return carry

    lax.fori_loop(0, experts, expert, 0)
    columns = lax.broadcasted_iota(jnp.int32, (GROUP * top, experts * GROUP), 1)

    def group(g, carry):
        first = pl.multiple_of(g * GROUP, GROUP)
        start = pl.multiple_of(g * (GROUP * top), GROUP * top)
        sel = (want_ref[pl.ds(start, GROUP * top), :] == columns).astype(F32).astype(BF)
        for kind in range(3):
            dense = p_ref[kind, :, pl.ds(first, GROUP), :].reshape(experts * GROUP, hidden)
            rows = dot(sel, dense).astype(BF)
            for pair in range(top // 2):
                lo = rows[2 * pair * GROUP : (2 * pair + 1) * GROUP]
                hi = rows[(2 * pair + 1) * GROUP : (2 * pair + 2) * GROUP]
                at = (kind * top + 2 * pair) * hidden
                out_ref[pl.ds(first, GROUP), at : at + 2 * hidden] = jnp.concatenate([lo, hi], axis=1)
        return carry

    lax.fori_loop(0, tokens // GROUP, group, 0)


def post_kernel(
    h_ref, xc_ref, want_ref, wg_ref, wu_ref, wd_ref, yx_ref, dg_ref, du_ref, dd_ref, hd_ref, acc_ref, y_ref
):
    experts = wg_ref.shape[0]
    pair_rows = wg_ref.shape[1]
    features = 2 * pair_rows
    hidden = wg_ref.shape[2] // 2
    tokens = xc_ref.shape[0]
    top = want_ref.shape[2] // GROUP
    step = pl.program_id(0)
    perm = pairing(features, False)
    back = pairing(features, True)
    x = dot(xc_ref[:, :features], perm).astype(BF)
    c = dot(xc_ref[:, features:], perm).astype(BF)
    slots = lax.broadcasted_iota(jnp.int32, (experts * GROUP, GROUP * top), 0)

    @pl.when(step == 0)
    def _():
        acc_ref[...] = jnp.zeros_like(acc_ref)

    y_ref[...] = jnp.zeros_like(y_ref)

    def group(g, carry):
        first = pl.multiple_of(g * GROUP, GROUP)
        sel = (slots == want_ref[g]).astype(F32).astype(BF)
        for kind in range(3):
            parts = []
            for pair in range(top // 2):
                at = (kind * top + 2 * pair) * hidden
                both = h_ref[pl.ds(first, GROUP), at : at + 2 * hidden]
                parts += [both[:, :hidden], both[:, hidden:]]
            dense = dot(sel, jnp.concatenate(parts, axis=0)).astype(BF)
            hd_ref[kind, :, pl.ds(first, GROUP), :] = dense.reshape(experts, GROUP, hidden)
        return carry

    lax.fori_loop(0, tokens // GROUP, group, 0)

    def expert(e, carry):
        value, gate_g, up_g = hd_ref[0, e], hd_ref[1, e], hd_ref[2, e]
        across = ((1,), (1,))
        y_ref[0] += dot(value, stacked(wd_ref[e]), across)
        y_ref[1] += dot(gate_g, stacked(wg_ref[e]), across) + dot(up_g, stacked(wu_ref[e]), across)
        down = ((0,), (0,))
        acc_ref[0, e] += dot(x, gate_g, down)
        acc_ref[1, e] += dot(x, up_g, down)
        acc_ref[2, e] += dot(c, value, down)
        return carry

    lax.fori_loop(0, experts, expert, 0)
    yx_ref[:, :features] = dot(y_ref[0].astype(BF), back).astype(BF)
    yx_ref[:, features:] = dot(y_ref[1].astype(BF), back).astype(BF)

    @pl.when(step == pl.num_programs(0) - 1)
    def _():
        def write(e, carry):
            for kind, d_ref in enumerate((dg_ref, du_ref, dd_ref)):
                total = acc_ref[kind, e].astype(BF)
                d_ref[e] = jnp.concatenate([total[:pair_rows], total[pair_rows:]], axis=1)
            return carry

        lax.fori_loop(0, experts, write, 0)


def whole(shape):
    return pl.BlockSpec(shape, lambda b: (0,) * len(shape))


def rows_of(shape):
    return pl.BlockSpec(shape, lambda b: (b,) + (0,) * (len(shape) - 1))


def params():
    return pltpu.CompilerParams(vmem_limit_bytes=58 * 2**20, dimension_semantics=("arbitrary",))


def shards(
    tokens_in, route_ids, route_gates, cotangent, gate_proj, up_proj, down_proj, replica_plan, capacity
):
    n = lax.axis_size("expert")
    source = lax.axis_index("expert")
    micro, tok, top = route_ids.shape
    experts, pair_rows, width = gate_proj.shape
    hidden = width // 2
    features = 2 * pair_rows
    local = micro * tok
    total = n * local
    block = min(total // 2, max(GROUP, 4096 // experts))
    blocks = total // block

    both = jnp.stack([tokens_in.reshape(local, -1), cotangent.reshape(local, -1)])
    full = lax.all_gather(both, "dp", axis=2, tiled=True)
    full = full.reshape(2, local, n, features).transpose(2, 1, 0, 3).reshape(n, local, 2 * features)
    xc = lax.all_to_all(full, "expert", split_axis=0, concat_axis=0, tiled=True)
    xc = xc.reshape(total, 2 * features)

    ids = lax.all_gather(route_ids.reshape(local, top), "expert", axis=0, tiled=True)
    want = ids.reshape(total // GROUP, GROUP, top) * GROUP
    want = want + jnp.arange(GROUP, dtype=jnp.int32)[None, :, None]
    want = want.transpose(0, 2, 1).reshape(total // GROUP, top * GROUP)

    weights = (gate_proj, up_proj, down_proj)
    partial_rows = pl.pallas_call(
        pre_kernel,
        grid=(blocks,),
        in_specs=[rows_of((block, 2 * features)), rows_of((block * top, 1))] + [whole(gate_proj.shape)] * 3,
        out_specs=rows_of((block, 3 * top * hidden)),
        out_shape=jax.ShapeDtypeStruct((total, 3 * top * hidden), BF),
        scratch_shapes=[pltpu.VMEM((3, experts, block, hidden), BF)],
        compiler_params=params(),
    )(xc, want.reshape(-1, 1), *weights)

    kept = jnp.stack(
        [kept_routes(route_ids[m], replica_plan[m], capacity[m], source, n) for m in range(micro)]
    ).reshape(local, top)
    spread = jnp.repeat(jnp.eye(top, dtype=F32), hidden, axis=1)
    kept_gate = jnp.where(kept, route_gates.reshape(local, top), 0.0)
    scale = jnp.dot(kept_gate, spread, precision=lax.Precision.HIGHEST)

    arrived = lax.all_to_all(
        partial_rows.reshape(n, local, -1), "expert", split_axis=0, concat_axis=0, tiled=True
    )
    sums = jnp.sum(arrived.astype(F32), axis=0)
    span = top * hidden
    pre_gate, pre_up, value = sums[:, :span], sums[:, span : 2 * span], sums[:, 2 * span :]
    logistic = jax.nn.sigmoid(pre_gate)
    swished = pre_gate * logistic
    value = value * scale
    mine = jnp.concatenate(
        [
            (swished * pre_up * scale).astype(BF),
            (value * pre_up * logistic * (1.0 + pre_gate * (1.0 - logistic))).astype(BF),
            (value * swished).astype(BF),
        ],
        axis=1,
    )
    everyone = lax.all_gather(mine, "expert", axis=0, tiled=True)

    yx, gate_grad, up_grad, down_grad = pl.pallas_call(
        post_kernel,
        grid=(blocks,),
        in_specs=[
            rows_of((block, 3 * span)),
            rows_of((block, 2 * features)),
            rows_of((block // GROUP, 1, top * GROUP)),
        ]
        + [whole(gate_proj.shape)] * 3,
        out_specs=[rows_of((block, 2 * features))] + [whole(gate_proj.shape)] * 3,
        out_shape=[jax.ShapeDtypeStruct((total, 2 * features), BF)]
        + [jax.ShapeDtypeStruct(gate_proj.shape, BF)] * 3,
        scratch_shapes=[
            pltpu.VMEM((3, experts, block, hidden), BF),
            pltpu.VMEM((3, experts, features, hidden), F32),
            pltpu.VMEM((2, block, features), F32),
        ],
        compiler_params=params(),
    )(everyone, xc, want.reshape(-1, 1, top * GROUP), *weights)

    home = lax.all_to_all(
        yx.reshape(n, local, 2 * features), "expert", split_axis=0, concat_axis=0, tiled=True
    )
    done = lax.psum_scatter(home, "dp", scatter_dimension=0, tiled=True)
    done = done.reshape(-1, local, 2, features).transpose(2, 1, 0, 3).reshape(2, micro, tok, -1)
    return done[0], done[1], gate_grad, up_grad, down_grad


def solution(mesh):
    split = P(None, "expert", "dp")
    tokens = P(None, "expert", None)
    in_specs = (split, tokens, tokens, split, split, split, split, P(), P())
    return jax.shard_map(shards, mesh=mesh, in_specs=in_specs, out_specs=(split,) * 5, check_vma=False)
```

profile of v0, /device:TPU:14, one launch (start us, length us, event | category | flops | bytes accessed | tf_op | source)
XLA Modules:
  0.0 357.1 jit_solution(16562593819094072698)
XLA Ops:
  7.2 0.9 pad_maximum_fusion.1
  8.1 6.8 %all_gather.9 = bf16[2,64,2048]{2,1,0:T(8,128)(2,1)S(1)} all-gather(bf16[2,64,512]{2,1,0:T(8,128)(2,1)S(1)} %pad_maximum_fusion.1), channel_id=1, replica_groups=mesh['dp'=4,'expert'=8] {'dp'}, dimensions={2}, use_global_device_ids=true | all-gather | bytes 655360 | tf_op jit(solution)/shard_map/all_gather | solution.py:177
  14.8 0.1 copy.62
  15.0 0.5 copy.65
  15.5 1.1 reshape.218
  16.6 6.2 %all-to-all-start = ((bf16[8,64,512]{2,1,0:T(8,128)(2,1)}), bf16[8,64,512]{2,1,0:T(8,128)(2,1)S(1)}, u32[]{:S(2)}, u32[]{:S(2)}) async-start(bf16[8,64,512]{2,1,0:T(8,128)(2,1)} %reshape.218), calls=%async_computation | async-start | bytes 1048576 | tf_op jit(solution)/shard_map/all_to_all | solution.py:179
  22.9 0.1 reshape.227
  23.0 31.6 %all-gather = s32[8,64,8]{1,2,0:T(8,128)S(1)} all-gather(s32[1,64,8]{1,2,0:T(8,128)S(1)} %reshape.227), channel_id=1, replica_groups=mesh['dp'=4,'expert'=8] {'expert'}, dimensions={0}, use_global_device_ids=true | all-gather | bytes 18432 | tf_op jit(solution)/shard_map/all_gather | solution.py:182
  54.6 0.1 mul.106
  54.7 0.1 copy.50
  54.7 2.5 reshape_reshape.8.want_ref
  57.3 0.8 copy-done
  58.1 25.5 %shard_map.128 = bf16[512,4608]{1,0:T(8,128)(2,1)} custom-call(bf16[512,512]{1,0:T(8,128)(2,1)} %bitcast.43, s32[4096,1]{1,0:T(8,128)} %reshape_reshape.8.want_ref, bf16[16,128,384]{2,1,0:T(8,128)(2,1)} %wg_ref.3, bf16[16,128,384]{2,1,0:T(8,128)(2,1)} %wu_ref.3, bf16[16,128,384]{2,1,0:T(8,128)(2,1)} %wd_ref.3), custom_call_target="tpu_custom_call" | custom-call | tf_op jit(solution)/shard_map/pallas_call | solution.py:188
  83.5 10.5 %all-to-all-start.1 = ((bf16[8,64,4608]{2,1,0:T(8,128)(2,1)}), bf16[8,64,4608]{2,1,0:T(8,128)(2,1)}, u32[]{:S(2)}, u32[]{:S(2)}) async-start(bf16[8,64,4608]{2,1,0:T(8,128)(2,1)} %bitcast.42), calls=%async_computation.1 | async-start | bytes 9437184 | tf_op jit(solution)/shard_map/all_to_all | solution.py:205
  94.1 0.1 rem.37
  94.2 0.1 convert_reduce_fusion.4
  94.3 0.1 convert_reduce_fusion.3
  94.4 0.1 select_reduce_fusion
  94.6 0.1 copy.56
  94.7 0.1 reduce_sum.78
  94.7 0.1 copy.53
  94.8 0.1 reduce_sum.73
  94.9 0.1 copy.55
  95.0 0.1 mul.118
  95.1 0.1 copy.52
  95.2 0.1 mul.110
  95.3 0.1 fusion.4
  95.4 0.2 convert_reduce_fusion.1
  95.6 0.1 reshape.223
  95.7 0.2 convert_reduce_fusion.2
  95.9 0.1 reshape.222
  96.1 0.1 select_n.59
  96.3 0.1 reshape.224
  96.4 93.2 %all-to-all-done.1 = bf16[8,64,4608]{2,1,0:T(8,128)(2,1)} async-done(((bf16[8,64,4608]{2,1,0:T(8,128)(2,1)}), bf16[8,64,4608]{2,1,0:T(8,128)(2,1)}, u32[]{:S(2)}, u32[]{:S(2)}) %all-to-all-start.1) | async-done | bytes 4718624 | tf_op jit(solution)/shard_map/all_to_all | solution.py:205
  189.6 3.1 convert_reduce_fusion
  192.7 0.7 multiply_convert_fusion.2
  193.4 0.9 pad_maximum_fusion
  194.3 0.1 copy.59
  194.4 0.7 copy.60.want_ref
  195.1 79.2 %all-gather.3.cloned.1.call-done.h_ref = bf16[512,4608]{1,0:T(8,128)(2,1)} async-done(((bf16[64,4608]{1,0:T(8,128)(2,1)}), bf16[512,4608]{1,0:T(8,128)(2,1)}) %all-gather.3.cloned.1.call-update) | async-done | bytes 4718608 | tf_op jit(solution)/shard_map/all_gather | solution.py:222
  274.3 33.7 %shard_map.129 = (bf16[512,512]{1,0:T(8,128)(2,1)}, bf16[16,128,384]{2,1,0:T(8,128)(2,1)}, bf16[16,128,384]{2,1,0:T(8,128)(2,1)}, bf16[16,128,384]{2,1,0:T(8,128)(2,1)}) custom-call(bf16[512,4608]{1,0:T(8,128)(2,1)} %all-gather.3.cloned.1.call-done.h_ref, bf16[512,512]{1,0:T(8,128)(2,1)} %bitcast.44, s32[32,1,128]{2,1,0:T(1,128)} %copy.60.want_ref, ...), custom_call_target="tpu_custom_call" | custom-call | tf_op jit(solution)/shard_map/pallas_call | solution.py:224
  308.0 18.2 %all_to_all.15 = bf16[8,64,512]{2,1,0:T(8,128)(2,1)} all-to-all(bf16[8,64,512]{2,1,0:T(8,128)(2,1)} %bitcast.48), channel_id=1, replica_groups=mesh['dp'=4,'expert'=8] {'expert'}, dimensions={0} | all-to-all | bytes 1048576 | tf_op jit(solution)/shard_map/all_to_all | solution.py:244
  326.2 21.5 %reduce-scatter.2.cloned.1.call-done = bf16[2,64,512]{2,1,0:T(8,128)(2,1)} async-done(((bf16[8,64,512]{2,1,0:T(8,128)(2,1)}), bf16[2,64,512]{2,1,0:T(8,128)(2,1)}) %reduce-scatter.2.cloned.1.call-update) | async-done | bytes 131088 | tf_op jit(solution)/shard_map/reduce_scatter | solution.py:247
  347.7 0.9 reshape.226
  348.7 0.1 copy.66
  348.8 0.1 fusion.6
  348.9 0.7 squeeze.5
  349.6 0.7 squeeze.4
  (33 shorter events, 0.5 us)
Async XLA Ops:
  15.0 7.9 %copy-start.1 = (s32[2,32,8]{1,2,0:T(8,128)S(1)}, s32[2,32,8]{1,2,0:T(8,128)}, u32[]{:S(2)}) copy-start(s32[2,32,8]{1,2,0:T(8,128)} %param.10) | copy-start | bytes 6148
  16.6 40.6 %all-to-all-start = ((bf16[8,64,512]{2,1,0:T(8,128)(2,1)}), bf16[8,64,512]{2,1,0:T(8,128)(2,1)S(1)}, u32[]{:S(2)}, u32[]{:S(2)}) async-start(bf16[8,64,512]{2,1,0:T(8,128)(2,1)} %reshape.218), calls=%async_computation | async-start | bytes 1048576 | tf_op jit(solution)/shard_map/all_to_all | solution.py:179
  57.3 0.8 copy-start
  83.5 10.7 %copy-start.3 = (s32[2,8]{1,0:T(2,128)S(1)}, s32[2,8]{1,0:T(2,128)}, u32[]{:S(2)}) copy-start(s32[2,8]{1,0:T(2,128)} %param.16) | copy-start | bytes 196
  83.5 10.9 %copy-start.4 = (s32[2,16]{1,0:T(2,128)S(1)}, s32[2,16]{1,0:T(2,128)}, u32[]{:S(2)}) copy-start(s32[2,16]{1,0:T(2,128)} %param.17) | copy-start | bytes 388
  83.5 12.6 %copy-start.2 = (f32[2,32,8]{1,2,0:T(8,128)S(1)}, f32[2,32,8]{1,2,0:T(8,128)}, u32[]{:S(2)}) copy-start(f32[2,32,8]{1,2,0:T(8,128)} %param.11) | copy-start | bytes 6148
  83.5 106.0 %all-to-all-start.1 = ((bf16[8,64,4608]{2,1,0:T(8,128)(2,1)}), bf16[8,64,4608]{2,1,0:T(8,128)(2,1)}, u32[]{:S(2)}, u32[]{:S(2)}) async-start(bf16[8,64,4608]{2,1,0:T(8,128)(2,1)} %bitcast.42), calls=%async_computation.1 | async-start | bytes 9437184 | tf_op jit(solution)/shard_map/all_to_all | solution.py:205
  94.0 180.3 %all-gather.3.cloned.1.call-start = ((), (), s32[]{:S(2)}) async-start(), calls=%async_computation.4 | async-start | bytes 5308416 | tf_op jit(solution)/shard_map/all_gather | solution.py:222
  194.3 153.4 %reduce-scatter.2.cloned.1.call-start = ((), (), s32[]{:S(2)}) async-start(), calls=%async_computation.5 | async-start | bytes 655360 | tf_op jit(solution)/shard_map/reduce_scatter | solution.py:247
Sparse Core Ops, SparseCore 0:
  194.4 79.8 all-gather.2
  326.4 21.3 reduce-scatter.1
where the time goes:
time: 360 us; the launch traced here: 357 us
  waiting for transfers between devices  194 us (54%)
  Pallas kernels  59.2 us (16%)
  blocking collectives  56.6 us (16%)
  starting transfers between devices  16.8 us (5%)
  between operations  14.2 us (4%)
  local copies, waits for them, and re-layouts  10 us (3%)
  other arithmetic  5.74 us (2%)
    all_to_all x1, waiting for transfers between devices, shards(): lax.all_to_all(partial_rows.reshape(n, local, -1), 'expert', split_axis=0...  93.2 us
    all_gather x1, waiting for transfers between devices, shards(): everyone = lax.all_gather(mine, 'expert', axis=0, tiled=True)  79.2 us
    pallas_call x1, Pallas kernels, shards(): pl.pallas_call(post_kernel, grid=(blocks,), in_specs=[rows_of((block, 3 *...  33.7 us
    all_gather x1, blocking collectives, shards(): lax.all_gather(route_ids.reshape(local, top), 'expert', axis=0, tiled=True)  31.6 us
    pallas_call x1, Pallas kernels, shards(): pl.pallas_call(pre_kernel, grid=(blocks,), in_specs=[rows_of((block, 2 *...  25.5 us
    reduce_scatter x1, waiting for transfers between devices, shards(): done = lax.psum_scatter(home, 'dp', scatter_dimension=0, tiled=True)  21.5 us
    all_to_all x1, blocking collectives, shards(): lax.all_to_all(yx.reshape(n, local, 2 * features), 'expert', split_axis=0...  18.2 us
    all_to_all x1, starting transfers between devices, shards(): lax.all_to_all(partial_rows.reshape(n, local, -1), 'expert', split_axis=0...  10.5 us
  transfers between devices with their start and end apart: 4, of which 3 were waited for; matrix products, arithmetic and copies ran while one was open for 2% of the time, Pallas kernels for 0%

commit v1 on v0

--- a/solution.py
+++ b/solution.py
@@ -54,7 +54,7 @@
     features = 2 * wg_ref.shape[1]
     hidden = wg_ref.shape[2] // 2
     tokens = xc_ref.shape[0]
-    top = want_ref.shape[0] // tokens
+    top = want_ref.shape[2] // GROUP
     perm = pairing(features, False)
     x = dot(xc_ref[:, :features], perm).astype(BF)
     c = dot(xc_ref[:, features:], perm).astype(BF)
@@ -65,15 +65,14 @@
         return carry
 
     lax.fori_loop(0, experts, expert, 0)
-    columns = lax.broadcasted_iota(jnp.int32, (GROUP * top, experts * GROUP), 1)
+    slots = lax.broadcasted_iota(jnp.int32, (experts * GROUP, GROUP * top), 0)
 
     def group(g, carry):
         first = pl.multiple_of(g * GROUP, GROUP)
-        start = pl.multiple_of(g * (GROUP * top), GROUP * top)
-        sel = (want_ref[pl.ds(start, GROUP * top), :] == columns).astype(F32).astype(BF)
+        sel = (slots == want_ref[g]).astype(F32).astype(BF)
         for kind in range(3):
             dense = p_ref[kind, :, pl.ds(first, GROUP), :].reshape(experts * GROUP, hidden)
-            rows = dot(sel, dense).astype(BF)
+            rows = dot(sel, dense, ((0,), (0,))).astype(BF)
             for pair in range(top // 2):
                 lo = rows[2 * pair * GROUP : (2 * pair + 1) * GROUP]
                 hi = rows[(2 * pair + 1) * GROUP : (2 * pair + 2) * GROUP]
@@ -147,6 +146,177 @@
         lax.fori_loop(0, experts, write, 0)
 
 
+def remote(src, dst, send_sem, recv_sem, dp, expert):
+    return pltpu.make_async_remote_copy(
+        src_ref=src,
+        dst_ref=dst,
+        send_sem=send_sem,
+        recv_sem=recv_sem,
+        device_id=(dp, expert),
+        device_id_type=pl.DeviceIdType.MESH,
+    )
+
+
+def greet(senders, count):
+    barrier = pltpu.get_barrier_semaphore()
+    for condition, dp, expert in senders:
+
+        @pl.when(condition)
+        def _():
+            pl.semaphore_signal(
+                barrier, inc=1, device_id=(dp, expert), device_id_type=pl.DeviceIdType.MESH
+            )
+
+    pl.semaphore_wait(barrier, count)
+
+
+def scatter_kernel(n, dpn, send_ref, want_ref, out_ref, ids_ref, local_sem, send_sem, recv_sem):
+    p, i = lax.axis_index("dp"), lax.axis_index("expert")
+    share = n // dpn
+    owner = i // share
+    selfish = owner == p
+    greet([((owner != p) | (k != i), owner, k) for k in range(n)], n - selfish.astype(jnp.int32))
+    targets = [(q, share * p + s, s, q * share + s) for q in range(dpn) for s in range(share)]
+
+    def copies(q, j, s, slot):
+        return (
+            remote(send_ref.at[s], out_ref.at[i], send_sem.at[0, slot], recv_sem.at[0, i], q, j),
+            remote(want_ref, ids_ref.at[i], send_sem.at[1, slot], recv_sem.at[1, i], q, j),
+        )
+
+    def own():
+        return (
+            pltpu.make_async_copy(send_ref.at[i % share], out_ref.at[i], local_sem.at[0]),
+            pltpu.make_async_copy(want_ref, ids_ref.at[i], local_sem.at[1]),
+        )
+
+    for q, j, s, slot in targets:
+
+        @pl.when((q != p) | (j != i))
+        def _():
+            for copy in copies(q, j, s, slot):
+                copy.start()
+
+    @pl.when(selfish)
+    def _():
+        for copy in own():
+            copy.start()
+
+    for k in range(n):
+
+        @pl.when((owner != p) | (k != i))
+        def _():
+            remote(send_ref.at[0], out_ref.at[k], send_sem.at[0, 0], recv_sem.at[0, k], owner, k).wait_recv()
+            remote(want_ref, ids_ref.at[k], send_sem.at[1, 0], recv_sem.at[1, k], owner, k).wait_recv()
+
+    for q, j, s, slot in targets:
+
+        @pl.when((q != p) | (j != i))
+        def _():
+            for copy in copies(q, j, s, slot):
+                copy.wait_send()
+
+    @pl.when(selfish)
+    def _():
+        for copy in own():
+            copy.wait()
+
+
+def collect_kernel(n, dpn, yx_ref, out_ref, buf_ref, local_sem, send_sem, recv_sem):
+    p, i = lax.axis_index("dp"), lax.axis_index("expert")
+    share = n // dpn
+    owner = i // share
+    selfish = owner == p
+    senders = [(q, share * p + s, q * share + s) for q in range(dpn) for s in range(share)]
+    greet([((q != p) | (j != i), q, j) for q, j, slot in senders], n - selfish.astype(jnp.int32))
+    mine = p * share + i % share
+
+    def copy(k):
+        return remote(yx_ref.at[k], buf_ref.at[mine], send_sem.at[k], recv_sem.at[mine], owner, k)
+
+    for k in range(n):
+
+        @pl.when((owner != p) | (k != i))
+        def _():
+            copy(k).start()
+
+    @pl.when(selfish)
+    def _():
+        own = pltpu.make_async_copy(yx_ref.at[i], buf_ref.at[mine], local_sem)
+        own.start()
+        own.wait()
+
+    for q, j, slot in senders:
+
+        @pl.when((q != p) | (j != i))
+        def _():
+            remote(yx_ref.at[0], buf_ref.at[slot], send_sem.at[0], recv_sem.at[slot], q, j).wait_recv()
+
+    features = yx_ref.shape[2] // 2
+    for s in range(share):
+        total = sum(buf_ref[q * share + s].astype(F32) for q in range(dpn)).astype(BF)
+        for kind in range(2):
+            out_ref[kind, :, s * features : (s + 1) * features] = total[:, kind * features : (kind + 1) * features]
+
+    for k in range(n):
+
+        @pl.when((owner != p) | (k != i))
+        def _():
+            copy(k).wait_send()
+
+
+def gather_kernel(n, in_ref, out_ref, local_sem, send_sem, recv_sem):
+    p, i = lax.axis_index("dp"), lax.axis_index("expert")
+    line = n // 2
+    a, b = i // 2, i % 2
+    other = a * 2 + 1 - b
+    always = a >= 0
+    has_left, has_right = a > 0, a < line - 1
+    greet(
+        [(always, p, other), (has_left, p, i - 2), (has_right, p, i + 2)],
+        1 + has_left.astype(jnp.int32) + has_right.astype(jnp.int32),
+    )
+    own = pltpu.make_async_copy(in_ref, out_ref.at[i], local_sem)
+    own.start()
+    started = []
+
+    def send(condition, src, chunk, target):
+        copy = remote(src, out_ref.at[chunk], send_sem.at[len(started)], recv_sem.at[chunk], p, target)
+        started.append((condition, copy))
+        pl.when(condition)(copy.start)
+
+    def arrive(condition, chunk):
+        copy = remote(in_ref, out_ref.at[chunk], send_sem.at[0], recv_sem.at[chunk], p, other)
+        pl.when(condition)(copy.wait_recv)
+
+    send(has_right, in_ref, i, i + 2)
+    send(has_left, in_ref, i, i - 2)
+    send(always, in_ref, i, other)
+    for step in range(1, line):
+        for sign in (-1, 1):
+            from_there = (a >= step) if sign < 0 else (a + step < line)
+            further = has_right if sign < 0 else has_left
+            chunk = jnp.where(from_there, i + 2 * sign * step, i)
+            arrive(from_there, chunk)
+            send(from_there & further, out_ref.at[chunk], chunk, i - 2 * sign)
+            send(from_there, out_ref.at[chunk], chunk, other)
+    for k in range(line):
+        arrive(always, 2 * k + 1 - b)
+    for condition, copy in started:
+        pl.when(condition)(copy.wait_send)
+    own.wait()
+
+
+def comm_params(number):
+    return pltpu.CompilerParams(
+        collective_id=number, has_side_effects=True, vmem_limit_bytes=58 * 2**20
+    )
+
+
+ANY = pl.BlockSpec(memory_space=pl.ANY)
+DMA = pltpu.SemaphoreType.DMA
+
+
 def whole(shape):
     return pl.BlockSpec(shape, lambda b: (0,) * len(shape))
 
@@ -173,27 +343,47 @@
     block = min(total // 2, max(GROUP, 4096 // experts))
     blocks = total // block
 
-    both = jnp.stack([tokens_in.reshape(local, -1), cotangent.reshape(local, -1)])
-    full = lax.all_gather(both, "dp", axis=2, tiled=True)
-    full = full.reshape(2, local, n, features).transpose(2, 1, 0, 3).reshape(n, local, 2 * features)
-    xc = lax.all_to_all(full, "expert", split_axis=0, concat_axis=0, tiled=True)
+    dpn = lax.axis_size("dp")
+    direct = n <= 16 and n % dpn == 0 and n % 2 == 0
+
+    want = route_ids.reshape(local // GROUP, GROUP, top) * GROUP
+    want = want + jnp.arange(GROUP, dtype=jnp.int32)[None, :, None]
+    want = want.transpose(0, 2, 1).reshape(local // GROUP, top * GROUP)
+    if direct:
+        share = n // dpn
+        both = jnp.stack([tokens_in.reshape(local, share, -1), cotangent.reshape(local, share, -1)])
+        both = both.transpose(2, 1, 0, 3).reshape(share, local, 2 * features)
+        xc, want = pl.pallas_call(
+            functools.partial(scatter_kernel, n, dpn),
+            in_specs=[ANY, ANY],
+            out_specs=[ANY, ANY],
+            out_shape=[
+                jax.ShapeDtypeStruct((n, local, 2 * features), BF),
+                jax.ShapeDtypeStruct((n,) + want.shape, jnp.int32),
+            ],
+            scratch_shapes=[DMA((2,)), DMA((2, n)), DMA((2, n))],
+            compiler_params=comm_params(0),
+        )(both, want)
+    else:
+        both = jnp.stack([tokens_in.reshape(local, -1), cotangent.reshape(local, -1)])
+        full = lax.all_gather(both, "dp", axis=2, tiled=True)
+        full = full.reshape(2, local, n, features).transpose(2, 1, 0, 3).reshape(n, local, 2 * features)
+        xc = lax.all_to_all(full, "expert", split_axis=0, concat_axis=0, tiled=True)
+        want = lax.all_gather(want, "expert", axis=0, tiled=True)
     xc = xc.reshape(total, 2 * features)
-
-    ids = lax.all_gather(route_ids.reshape(local, top), "expert", axis=0, tiled=True)
-    want = ids.reshape(total // GROUP, GROUP, top) * GROUP
-    want = want + jnp.arange(GROUP, dtype=jnp.int32)[None, :, None]
-    want = want.transpose(0, 2, 1).reshape(total // GROUP, top * GROUP)
+    want = want.reshape(total // GROUP, 1, top * GROUP)
 
     weights = (gate_proj, up_proj, down_proj)
     partial_rows = pl.pallas_call(
         pre_kernel,
         grid=(blocks,),
-        in_specs=[rows_of((block, 2 * features)), rows_of((block * top, 1))] + [whole(gate_proj.shape)] * 3,
+        in_specs=[rows_of((block, 2 * features)), rows_of((block // GROUP, 1, top * GROUP))]
+        + [whole(gate_proj.shape)] * 3,
         out_specs=rows_of((block, 3 * top * hidden)),
         out_shape=jax.ShapeDtypeStruct((total, 3 * top * hidden), BF),
         scratch_shapes=[pltpu.VMEM((3, experts, block, hidden), BF)],
         compiler_params=params(),
-    )(xc, want.reshape(-1, 1), *weights)
+    )(xc, want, *weights)
 
     kept = jnp.stack(
         [kept_routes(route_ids[m], replica_plan[m], capacity[m], source, n) for m in range(micro)]
@@ -219,7 +409,17 @@
         ],
         axis=1,
     )
-    everyone = lax.all_gather(mine, "expert", axis=0, tiled=True)
+    if direct:
+        everyone = pl.pallas_call(
+            functools.partial(gather_kernel, n),
+            in_specs=[ANY],
+            out_specs=ANY,
+            out_shape=jax.ShapeDtypeStruct((n, local, 3 * span), BF),
+            scratch_shapes=[DMA, DMA((2 * n + 8,)), DMA((n,))],
+            compiler_params=comm_params(1),
+        )(mine).reshape(total, 3 * span)
+    else:
+        everyone = lax.all_gather(mine, "expert", axis=0, tiled=True)
 
     yx, gate_grad, up_grad, down_grad = pl.pallas_call(
         post_kernel,
@@ -239,13 +439,23 @@
             pltpu.VMEM((2, block, features), F32),
         ],
         compiler_params=params(),
-    )(everyone, xc, want.reshape(-1, 1, top * GROUP), *weights)
-
-    home = lax.all_to_all(
-        yx.reshape(n, local, 2 * features), "expert", split_axis=0, concat_axis=0, tiled=True
-    )
-    done = lax.psum_scatter(home, "dp", scatter_dimension=0, tiled=True)
-    done = done.reshape(-1, local, 2, features).transpose(2, 1, 0, 3).reshape(2, micro, tok, -1)
+    )(everyone, xc, want, *weights)
+
+    yx = yx.reshape(n, local, 2 * features)
+    if direct:
+        done = pl.pallas_call(
+            functools.partial(collect_kernel, n, dpn),
+            in_specs=[ANY],
+            out_specs=pl.BlockSpec(memory_space=pltpu.VMEM),
+            out_shape=jax.ShapeDtypeStruct((2, local, n // dpn * features), BF),
+            scratch_shapes=[pltpu.VMEM((n, local, 2 * features), BF), DMA, DMA((n,)), DMA((n,))],
+            compiler_params=comm_params(2),
+        )(yx)
+    else:
+        home = lax.all_to_all(yx, "expert", split_axis=0, concat_axis=0, tiled=True)
+        done = lax.psum_scatter(home, "dp", scatter_dimension=0, tiled=True)
+        done = done.reshape(-1, local, 2, features).transpose(2, 1, 0, 3)
+    done = done.reshape(2, micro, tok, -1)
     return done[0], done[1], gate_grad, up_grad, down_grad
 
 

time: 360 us -> 283 us (0.79)
  Pallas kernels: 59.2 us -> 163 us
  waiting for transfers between devices: 194 us -> 100 us
  blocking collectives: 56.6 us -> 0 us
  between operations: 14.2 us -> 0.83 us
  starting transfers between devices: 16.8 us -> 5.96 us
  local copies, waits for them, and re-layouts: 10 us -> 6.37 us
    pallas_call x0 -> x3, Pallas kernels: none -> 104 us  [the longest x1 58.3 us: shards(): pl.pallas_call(functools.partial(gather_kernel, n), in_specs=[ANY], out_s...]
    all_gather x1 -> x0, waiting for transfers between devices: 79.2 us -> none  [shards(): everyone = lax.all_gather(mine, 'expert', axis=0, tiled=True)]
    all_gather x2 -> x0, blocking collectives: 38.4 us -> none  [the longest x1 31.6 us: shards(): lax.all_gather(route_ids.reshape(local, top), 'expert', axis=0, tiled=True)]
    reduce_scatter x1 -> x0, waiting for transfers between devices: 21.5 us -> none  [shards(): done = lax.psum_scatter(home, 'dp', scatter_dimension=0, tiled=True)]
    all_to_all x1 -> x0, blocking collectives: 18.2 us -> none  [shards(): lax.all_to_all(yx.reshape(n, local, 2 * features), 'expert', split_axis=0...]
    all_to_all x1, waiting for transfers between devices: 93.2 us -> 100 us  [shards(): lax.all_to_all(partial_rows.reshape(n, local, -1), 'expert', split_axis=0...]
    all_to_all x1 -> x0, starting transfers between devices: 6.22 us -> none  [shards(): xc = lax.all_to_all(full, 'expert', split_axis=0, concat_axis=0, tiled=True)]
    all_to_all x1, starting transfers between devices: 10.5 us -> 5.96 us  [shards(): lax.all_to_all(partial_rows.reshape(n, local, -1), 'expert', split_axis=0...]
  transfers between devices with their start and end apart: 4 -> 1, of which waited for: 3 -> 1; matrix products, arithmetic and copies ran while one was open for 2% -> 1% of each run, Pallas kernels for 0% -> 0%
where the time goes in v1:
time: 283 us; the launch traced here: 282 us
  Pallas kernels  163 us (58%)
  waiting for transfers between devices  100 us (35%)
  local copies, waits for them, and re-layouts  6.37 us (2%)
  starting transfers between devices  5.96 us (2%)
  other arithmetic  5.85 us (2%)
    all_to_all x1, waiting for transfers between devices, shards(): lax.all_to_all(partial_rows.reshape(n, local, -1), 'expert', split_axis=0...  100 us
    pallas_call x1, Pallas kernels, shards(): pl.pallas_call(functools.partial(gather_kernel, n), in_specs=[ANY], out_s...  58.3 us
    pallas_call x1, Pallas kernels, shards(): pl.pallas_call(post_kernel, grid=(blocks,), in_specs=[rows_of((block, 3 *...  33.7 us
    pallas_call x1, Pallas kernels, shards(): pl.pallas_call(functools.partial(scatter_kernel, n, dpn), in_specs=[ANY,...  26.1 us
    pallas_call x1, Pallas kernels, shards(): pl.pallas_call(pre_kernel, grid=(blocks,), in_specs=[rows_of((block, 2 *...  24.7 us
    pallas_call x1, Pallas kernels, shards(): pl.pallas_call(functools.partial(collect_kernel, n, dpn), in_specs=[ANY],...  19.7 us
    all_to_all x1, starting transfers between devices, shards(): lax.all_to_all(partial_rows.reshape(n, local, -1), 'expert', split_axis=0...  5.96 us
  transfers between devices with their start and end apart: 1, of which 1 were waited for; matrix products, arithmetic and copies ran while one was open for 1% of the time, Pallas kernels for 0%

profile of v1, /device:TPU:14, one launch (start us, length us, event | category | flops | bytes accessed | tf_op | source)
XLA Modules:
  0.0 282.3 jit_solution(7301674384362402820)
XLA Ops:
  0.6 0.7 broadcast_multiply_fusion
  1.3 0.1 mul.106
  1.4 0.7 reshape.218.want_ref
  2.1 0.9 stack_reshape.6
  3.0 0.1 copy.39
  3.1 0.9 stack_reshape.7
  3.9 0.1 copy.40
  4.1 0.3 maximum_bitcast_fusion
  4.4 0.7 reshape.217.send_ref
  5.1 26.1 %shard_map.128 = (bf16[8,64,512]{2,1,0:T(8,128)(2,1)}, s32[8,4,128]{2,1,0:T(4,128)}) custom-call(bf16[2,64,512]{2,1,0:T(8,128)(2,1)} %reshape.217.send_ref, s32[4,128]{1,0:T(4,128)} %reshape.218.want_ref), custom_call_target="tpu_custom_call" | custom-call | tf_op jit(solution)/shard_map/pallas_call | solution.py:356
  31.3 24.7 %shard_map.129 = bf16[512,4608]{1,0:T(8,128)(2,1)} custom-call(bf16[512,512]{1,0:T(8,128)(2,1)} %bitcast.35, s32[32,1,128]{2,1,0:T(1,128)} %bitcast.38, bf16[16,128,384]{2,1,0:T(8,128)(2,1)} %wg_ref.3, bf16[16,128,384]{2,1,0:T(8,128)(2,1)} %wu_ref.3, bf16[16,128,384]{2,1,0:T(8,128)(2,1)} %wd_ref.3), custom_call_target="tpu_custom_call" | custom-call | tf_op jit(solution)/shard_map/pallas_call | solution.py:377
  56.0 0.0 copy-start.1
  56.0 6.0 %all-to-all-start = ((bf16[8,64,4608]{2,1,0:T(8,128)(2,1)}), bf16[8,64,4608]{2,1,0:T(8,128)(2,1)}, u32[]{:S(2)}, u32[]{:S(2)}) async-start(bf16[8,64,4608]{2,1,0:T(8,128)(2,1)} %bitcast.33), calls=%async_computation | async-start | bytes 9437184 | tf_op jit(solution)/shard_map/all_to_all | solution.py:395
  62.0 0.1 rem.36
  62.1 0.1 rem.37
  62.2 0.0 copy-done.2
  62.2 0.1 convert_reduce_fusion.4
  62.3 0.1 convert_reduce_fusion.3
  62.4 0.0 copy-done.3
  62.4 0.0 copy-done
  62.4 0.1 select_reduce_fusion
  62.5 0.1 copy.47
  62.6 0.1 reduce_sum.78
  62.7 0.1 copy.44
  62.8 0.1 reduce_sum.73
  62.9 0.1 copy.46
  62.9 0.1 mul.118
  63.0 0.1 copy.43
  63.1 0.1 mul.110
  63.2 0.1 fusion.4
  63.3 0.2 convert_reduce_fusion.1
  63.5 0.1 reshape.223
  63.6 0.1 copy.48
  63.7 0.2 convert_reduce_fusion.2
  63.9 0.1 reshape.222
  64.0 0.1 copy.45
  64.1 0.0 copy-done.1
  64.1 0.1 select_n.59
  64.2 0.1 broadcast_in_dim.12
  64.3 0.1 reshape.224
  64.3 100.1 %all-to-all-done = bf16[8,64,4608]{2,1,0:T(8,128)(2,1)} async-done(((bf16[8,64,4608]{2,1,0:T(8,128)(2,1)}), bf16[8,64,4608]{2,1,0:T(8,128)(2,1)}, u32[]{:S(2)}, u32[]{:S(2)}) %all-to-all-start) | async-done | bytes 4718624 | tf_op jit(solution)/shard_map/all_to_all | solution.py:395
  164.5 3.1 %convert_reduce_fusion = f32[64,4608]{1,0:T(8,128)S(1)} fusion(bf16[8,64,4608]{2,1,0:T(8,128)(2,1)} %all-to-all-done), kind=kLoop, calls=%fused_computation | loop fusion | flops 4423680 | bytes 5898240 | tf_op jit(solution)/shard_map/reduce_sum | solution.py:398
  167.6 0.7 multiply_convert_fusion.2
  168.3 0.9 pad_maximum_fusion.in_ref
  169.1 58.3 %shard_map.130 = bf16[8,64,4608]{2,1,0:T(8,128)(2,1)} custom-call(bf16[64,4608]{1,0:T(8,128)(2,1)} %pad_maximum_fusion.in_ref), custom_call_target="tpu_custom_call" | custom-call | tf_op jit(solution)/shard_map/pallas_call | solution.py:413
  227.4 33.7 %shard_map.131 = (bf16[512,512]{1,0:T(8,128)(2,1)}, bf16[16,128,384]{2,1,0:T(8,128)(2,1)}, bf16[16,128,384]{2,1,0:T(8,128)(2,1)}, bf16[16,128,384]{2,1,0:T(8,128)(2,1)}) custom-call(bf16[512,4608]{1,0:T(8,128)(2,1)} %bitcast.34, bf16[512,512]{1,0:T(8,128)(2,1)} %bitcast.36, s32[32,1,128]{2,1,0:T(1,128)} %bitcast.39, bf16[16,128,384]{2,1,0:T(8,128)(2,1)} %wg_ref.3, ...), custom_call_target="tpu_custom_call" | custom-call | tf_op jit(solution)/shard_map/pallas_call | solution.py:424
  261.1 19.7 %shard_map.132 = bf16[2,64,512]{2,1,0:T(8,128)(2,1)} custom-call(bf16[8,64,512]{2,1,0:T(8,128)(2,1)} %bitcast.37), custom_call_target="tpu_custom_call" | custom-call | tf_op jit(solution)/shard_map/pallas_call | solution.py:446
  280.8 1.5 fusion.6
  (17 shorter events, 0.1 us)
Async XLA Ops:
  56.0 6.2 %copy-start.2 = (s32[2,8]{1,0:T(2,128)S(1)}, s32[2,8]{1,0:T(2,128)}, u32[]{:S(2)}) copy-start(s32[2,8]{1,0:T(2,128)} %param.16) | copy-start | bytes 196
  56.0 6.4 %copy-start.3 = (s32[2,16]{1,0:T(2,128)S(1)}, s32[2,16]{1,0:T(2,128)}, u32[]{:S(2)}) copy-start(s32[2,16]{1,0:T(2,128)} %param.17) | copy-start | bytes 388
  56.0 6.4 %copy-start = (s32[2,32,8]{1,2,0:T(8,128)S(1)}, s32[2,32,8]{1,2,0:T(8,128)}, u32[]{:S(2)}) copy-start(s32[2,32,8]{1,2,0:T(8,128)} %param.10) | copy-start | bytes 6148
  56.0 8.1 %copy-start.1 = (f32[2,32,8]{1,2,0:T(8,128)S(1)}, f32[2,32,8]{1,2,0:T(8,128)}, u32[]{:S(2)}) copy-start(f32[2,32,8]{1,2,0:T(8,128)} %param.11) | copy-start | bytes 6148
  56.0 108.4 %all-to-all-start = ((bf16[8,64,4608]{2,1,0:T(8,128)(2,1)}), bf16[8,64,4608]{2,1,0:T(8,128)(2,1)}, u32[]{:S(2)}, u32[]{:S(2)}) async-start(bf16[8,64,4608]{2,1,0:T(8,128)(2,1)} %bitcast.33), calls=%async_computation | async-start | bytes 9437184 | tf_op jit(solution)/shard_map/all_to_all | solution.py:395

commit v2 on v1

--- a/solution.py
+++ b/solution.py
@@ -95,8 +95,8 @@
     step = pl.program_id(0)
     perm = pairing(features, False)
     back = pairing(features, True)
-    x = dot(xc_ref[:, :features], perm).astype(BF)
-    c = dot(xc_ref[:, features:], perm).astype(BF)
+    x = dot(perm, xc_ref[:, :features], ((0,), (1,))).astype(BF)
+    c = dot(perm, xc_ref[:, features:], ((0,), (1,))).astype(BF)
     slots = lax.broadcasted_iota(jnp.int32, (experts * GROUP, GROUP * top), 0)
 
     @pl.when(step == 0)
@@ -125,10 +125,9 @@
         across = ((1,), (1,))
         y_ref[0] += dot(value, stacked(wd_ref[e]), across)
         y_ref[1] += dot(gate_g, stacked(wg_ref[e]), across) + dot(up_g, stacked(wu_ref[e]), across)
-        down = ((0,), (0,))
-        acc_ref[0, e] += dot(x, gate_g, down)
-        acc_ref[1, e] += dot(x, up_g, down)
-        acc_ref[2, e] += dot(c, value, down)
+        acc_ref[0, e] += dot(x, gate_g)
+        acc_ref[1, e] += dot(x, up_g)
+        acc_ref[2, e] += dot(c, value)
         return carry
 
     lax.fori_loop(0, experts, expert, 0)
@@ -263,6 +262,110 @@
         @pl.when((owner != p) | (k != i))
         def _():
             copy(k).wait_send()
+
+
+def activate(pre_gate, pre_up, value, scale):
+    logistic = jax.nn.sigmoid(pre_gate)
+    swished = pre_gate * logistic
+    value = value * scale
+    return (
+        (swished * pre_up * scale).astype(BF),
+        (value * pre_up * logistic * (1.0 + pre_gate * (1.0 - logistic))).astype(BF),
+        (value * swished).astype(BF),
+    )
+
+
+def reduce_kernel(
+    n, pieces, in_ref, scale_ref, out_ref, y_ref, stage_ref, z_ref, sum_ref, y_send, y_recv, z_send, z_recv
+):
+    p, i = lax.axis_index("dp"), lax.axis_index("expert")
+    line = n // 2
+    a, b = i // 2, i % 2
+    other = a * 2 + 1 - b
+    always = a >= 0
+    has_left, has_right = a > 0, a < line - 1
+    rows = in_ref.shape[1] // pieces
+    span = scale_ref.shape[1]
+    greet(
+        [(always, p, other), (has_left, p, i - 2), (has_right, p, i + 2)],
+        1 + has_left.astype(jnp.int32) + has_right.astype(jnp.int32),
+    )
+    order = []
+    for k in range((line + 1) // 2):
+        order += [line - 1 - k] if line - 1 - k == k else [line - 1 - k, k]
+
+    def across(h, d):
+        at = pl.ds(h * rows, rows)
+        return remote(
+            in_ref.at[2 * d + 1 - b, at], y_ref.at[d, at], y_send.at[h, d], y_recv.at[h, d], p, other
+        )
+
+    def along(h, d, side):
+        at = pl.ds(h * rows, rows)
+        target = i + 2 if side == 0 else i - 2
+        return remote(
+            stage_ref.at[d, at], z_ref.at[side, d, at], z_send.at[h, d], z_recv.at[side, h, d], p, target
+        )
+
+    def add(target, terms):
+        def body(k, carry):
+            at = pl.ds(pl.multiple_of(k * span, span), span)
+            total = terms[0][:, at].astype(F32)
+            for term in terms[1:]:
+                total = total + term[:, at].astype(F32)
+            target[:, at] = total.astype(target.dtype)
+            return carry
+
+        lax.fori_loop(0, 3, body, 0)
+
+    for h in range(pieces):
+        for d in order:
+            across(h, d).start()
+
+    for h in range(pieces):
+        at = pl.ds(h * rows, rows)
+        for d in order:
+            across(h, d).wait_recv()
+            both = [in_ref.at[2 * d + b, at], y_ref.at[d, at]]
+            for side in range(2):
+                passing = a < d if side == 0 else a > d
+                behind = has_left if side == 0 else has_right
+
+                @pl.when(passing)
+                def _():
+                    @pl.when(behind)
+                    def _():
+                        along(h, d, side).wait_recv()
+                        add(stage_ref.at[d, at], both + [z_ref.at[side, d, at]])
+
+                    @pl.when(jnp.logical_not(behind))
+                    def _():
+                        add(stage_ref.at[d, at], both)
+
+                    along(h, d, side).start()
+
+    for h in range(pieces):
+        at = pl.ds(h * rows, rows)
+        total = sum_ref.at[at]
+        add(total, [in_ref.at[i, at], y_ref.at[a, at]])
+        for side in range(2):
+
+            @pl.when(has_left if side == 0 else has_right)
+            def _():
+                along(h, a, side).wait_recv()
+                add(total, [total, z_ref.at[side, a, at]])
+
+        parts = activate(
+            sum_ref[at, :span], sum_ref[at, span : 2 * span], sum_ref[at, 2 * span :], scale_ref[at, :]
+        )
+        for kind, part in enumerate(parts):
+            out_ref[at, kind * span : (kind + 1) * span] = part
+
+    for h in range(pieces):
+        for d in order:
+            across(h, d).wait_send()
+            for side in range(2):
+                pl.when(a < d if side == 0 else a > d)(along(h, d, side).wait_send)
 
 
 def gather_kernel(n, in_ref, out_ref, local_sem, send_sem, recv_sem):
@@ -392,23 +495,34 @@
     kept_gate = jnp.where(kept, route_gates.reshape(local, top), 0.0)
     scale = jnp.dot(kept_gate, spread, precision=lax.Precision.HIGHEST)
 
-    arrived = lax.all_to_all(
-        partial_rows.reshape(n, local, -1), "expert", split_axis=0, concat_axis=0, tiled=True
-    )
-    sums = jnp.sum(arrived.astype(F32), axis=0)
     span = top * hidden
-    pre_gate, pre_up, value = sums[:, :span], sums[:, span : 2 * span], sums[:, 2 * span :]
-    logistic = jax.nn.sigmoid(pre_gate)
-    swished = pre_gate * logistic
-    value = value * scale
-    mine = jnp.concatenate(
-        [
-            (swished * pre_up * scale).astype(BF),
-            (value * pre_up * logistic * (1.0 + pre_gate * (1.0 - logistic))).astype(BF),
-            (value * swished).astype(BF),
-        ],
-        axis=1,
-    )
+    partial_rows = partial_rows.reshape(n, local, 3 * span)
+    if direct:
+        pieces = 2 if local % 32 == 0 else 1
+        slots = (n // 2, local, 3 * span)
+        vmem = pl.BlockSpec(memory_space=pltpu.VMEM)
+        mine = pl.pallas_call(
+            functools.partial(reduce_kernel, n, pieces),
+            in_specs=[vmem, vmem],
+            out_specs=vmem,
+            out_shape=jax.ShapeDtypeStruct((local, 3 * span), BF),
+            scratch_shapes=[
+                pltpu.VMEM(slots, BF),
+                pltpu.VMEM(slots, BF),
+                pltpu.VMEM((2,) + slots, BF),
+                pltpu.VMEM((local, 3 * span), F32),
+                DMA((pieces, n // 2)),
+                DMA((pieces, n // 2)),
+                DMA((pieces, n // 2)),
+                DMA((2, pieces, n // 2)),
+            ],
+            compiler_params=comm_params(3),
+        )(partial_rows, scale)
+    else:
+        arrived = lax.all_to_all(partial_rows, "expert", split_axis=0, concat_axis=0, tiled=True)
+        sums = jnp.sum(arrived.astype(F32), axis=0)
+        parts = activate(sums[:, :span], sums[:, span : 2 * span], sums[:, 2 * span :], scale)
+        mine = jnp.concatenate(parts, axis=1)
     if direct:
         everyone = pl.pallas_call(
             functools.partial(gather_kernel, n),

time: 283 us -> 245 us (0.87)
  waiting for transfers between devices: 100 us -> 0 us
  Pallas kernels: 163 us -> 231 us
  starting transfers between devices: 5.96 us -> 0 us
    all_to_all x1 -> x0, waiting for transfers between devices: 100 us -> none  [shards(): lax.all_to_all(partial_rows.reshape(n, local, -1), 'expert', split_axis=0...]
    pallas_call x0 -> x1, Pallas kernels: none -> 74.1 us  [shards(): pl.pallas_call(functools.partial(reduce_kernel, n, pieces), in_specs=[vme...]
    all_to_all x1 -> x0, starting transfers between devices: 5.96 us -> none  [shards(): lax.all_to_all(partial_rows.reshape(n, local, -1), 'expert', split_axis=0...]
    pallas_call x1, Pallas kernels: 58.3 us -> 54 us  [shards(): pl.pallas_call(functools.partial(gather_kernel, n), in_specs=[ANY], out_s...]
    reduce_sum x1 -> x0, other arithmetic: 3.14 us -> none  [shards(): sums = jnp.sum(arrived.astype(F32), axis=0)]
  transfers between devices with their start and end apart: 1 -> 0, of which waited for: 1 -> 0; matrix products, arithmetic and copies ran while one was open for 1% -> 0% of each run, Pallas kernels for 0% -> 0%
where the time goes in v2:
time: 245 us; the launch traced here: 244 us
  Pallas kernels  231 us (94%)
  local copies, waits for them, and re-layouts  7.87 us (3%)
  other arithmetic  3.26 us (1%)
    pallas_call x1, Pallas kernels, shards(): pl.pallas_call(functools.partial(reduce_kernel, n, pieces), in_specs=[vme...  74.1 us
    pallas_call x1, Pallas kernels, shards(): pl.pallas_call(functools.partial(gather_kernel, n), in_specs=[ANY], out_s...  54 us
    pallas_call x1, Pallas kernels, shards(): pl.pallas_call(post_kernel, grid=(blocks,), in_specs=[rows_of((block, 3 *...  33.7 us
    pallas_call x1, Pallas kernels, shards(): pl.pallas_call(functools.partial(scatter_kernel, n, dpn), in_specs=[ANY,...  26.1 us
    pallas_call x1, Pallas kernels, shards(): pl.pallas_call(pre_kernel, grid=(blocks,), in_specs=[rows_of((block, 2 *...  24.7 us
    pallas_call x1, Pallas kernels, shards(): pl.pallas_call(functools.partial(collect_kernel, n, dpn), in_specs=[ANY],...  18.7 us

profile of v2, /device:TPU:14, one launch (start us, length us, event | category | flops | bytes accessed | tf_op | source)
XLA Modules:
  0.0 244.4 jit_solution(2884496635329075588)
XLA Ops:
  0.6 0.8 slice_bitcast_fusion.5
  1.4 0.1 convert_reduce_fusion.3
  1.5 0.1 convert_reduce_fusion.2
  1.6 0.8 slice_bitcast_fusion.4
  2.4 0.7 broadcast_multiply_fusion
  3.1 0.1 mul.79
  3.2 0.7 reshape.218.want_ref
  3.8 0.1 rem.36
  3.9 0.1 rem.37
  4.0 0.7 slice_bitcast_fusion.1
  4.7 0.1 select_reduce_fusion
  4.8 0.1 copy.47
  4.9 0.1 reduce_sum.68
  5.0 0.1 copy.44
  5.1 0.1 reduce_sum.63
  5.2 0.1 copy.46
  5.2 0.1 mul.89
  5.3 0.1 copy.43
  5.4 0.1 mul.81
  5.5 0.1 fusion.3
  5.6 0.2 convert_reduce_fusion.1
  5.8 0.2 convert_reduce_fusion
  6.0 0.1 reshape.223
  6.1 0.1 copy.48
  6.2 0.1 reshape.222
  6.3 0.1 copy.45
  6.3 0.7 add_select_fusion
  7.1 0.1 select_n.59
  7.2 0.1 broadcast_in_dim.12
  7.2 0.1 reshape.224
  7.3 0.9 stack_reshape.6
  8.2 0.1 copy.39
  8.3 0.9 stack_reshape.7
  9.1 0.1 copy.40
  9.3 0.3 maximum_bitcast_fusion
  9.6 0.7 reshape.217.send_ref
  10.3 1.3 fusion.6.scale_ref
  11.6 26.1 %shard_map.128 = (bf16[8,64,512]{2,1,0:T(8,128)(2,1)}, s32[8,4,128]{2,1,0:T(4,128)}) custom-call(bf16[2,64,512]{2,1,0:T(8,128)(2,1)} %reshape.217.send_ref, s32[4,128]{1,0:T(4,128)} %reshape.218.want_ref), custom_call_target="tpu_custom_call" | custom-call | tf_op jit(solution)/shard_map/pallas_call | solution.py:459
  37.7 24.7 %shard_map.129 = bf16[512,4608]{1,0:T(8,128)(2,1)} custom-call(bf16[512,512]{1,0:T(8,128)(2,1)} %bitcast.35, s32[32,1,128]{2,1,0:T(1,128)} %bitcast.38, bf16[16,128,384]{2,1,0:T(8,128)(2,1)} %wg_ref.3, bf16[16,128,384]{2,1,0:T(8,128)(2,1)} %wu_ref.3, bf16[16,128,384]{2,1,0:T(8,128)(2,1)} %wd_ref.3), custom_call_target="tpu_custom_call" | custom-call | tf_op jit(solution)/shard_map/pallas_call | solution.py:480
  62.4 74.1 %shard_map.130.in_ref = bf16[64,4608]{1,0:T(8,128)(2,1)} custom-call(bf16[8,64,4608]{2,1,0:T(8,128)(2,1)} %bitcast.34, f32[64,1536]{1,0:T(8,128)} %fusion.6.scale_ref), custom_call_target="tpu_custom_call" | custom-call | tf_op jit(solution)/shard_map/pallas_call | solution.py:504
  136.5 54.0 %shard_map.131 = bf16[8,64,4608]{2,1,0:T(8,128)(2,1)} custom-call(bf16[64,4608]{1,0:T(8,128)(2,1)} %shard_map.130.in_ref), custom_call_target="tpu_custom_call" | custom-call | tf_op jit(solution)/shard_map/pallas_call | solution.py:527
  190.5 33.7 %shard_map.132 = (bf16[512,512]{1,0:T(8,128)(2,1)}, bf16[16,128,384]{2,1,0:T(8,128)(2,1)}, bf16[16,128,384]{2,1,0:T(8,128)(2,1)}, bf16[16,128,384]{2,1,0:T(8,128)(2,1)}) custom-call(bf16[512,4608]{1,0:T(8,128)(2,1)} %bitcast.33, bf16[512,512]{1,0:T(8,128)(2,1)} %bitcast.36, s32[32,1,128]{2,1,0:T(1,128)} %bitcast.39, bf16[16,128,384]{2,1,0:T(8,128)(2,1)} %wg_ref.3, ...), custom_call_target="tpu_custom_call" | custom-call | tf_op jit(solution)/shard_map/pallas_call | solution.py:538
  224.2 18.7 %shard_map.133 = bf16[2,64,512]{2,1,0:T(8,128)(2,1)} custom-call(bf16[8,64,512]{2,1,0:T(8,128)(2,1)} %bitcast.37), custom_call_target="tpu_custom_call" | custom-call | tf_op jit(solution)/shard_map/pallas_call | solution.py:560
  242.9 1.5 fusion.5
  (10 shorter events, 0.1 us)

commit v3 on v2

--- a/solution.py
+++ b/solution.py
@@ -64,7 +64,7 @@
             p_ref[kind, e] = dot(rows, stacked(w_ref[e])).astype(BF)
         return carry
 
-    lax.fori_loop(0, experts, expert, 0)
+    lax.fori_loop(0, experts, expert, 0, unroll=4)
     slots = lax.broadcasted_iota(jnp.int32, (experts * GROUP, GROUP * top), 0)
 
     def group(g, carry):
@@ -80,7 +80,7 @@
                 out_ref[pl.ds(first, GROUP), at : at + 2 * hidden] = jnp.concatenate([lo, hi], axis=1)
         return carry
 
-    lax.fori_loop(0, tokens // GROUP, group, 0)
+    lax.fori_loop(0, tokens // GROUP, group, 0, unroll=2)
 
 
 def post_kernel(
@@ -118,7 +118,7 @@
             hd_ref[kind, :, pl.ds(first, GROUP), :] = dense.reshape(experts, GROUP, hidden)
         return carry
 
-    lax.fori_loop(0, tokens // GROUP, group, 0)
+    lax.fori_loop(0, tokens // GROUP, group, 0, unroll=2)
 
     def expert(e, carry):
         value, gate_g, up_g = hd_ref[0, e], hd_ref[1, e], hd_ref[2, e]
@@ -130,7 +130,7 @@
         acc_ref[2, e] += dot(c, value)
         return carry
 
-    lax.fori_loop(0, experts, expert, 0)
+    lax.fori_loop(0, experts, expert, 0, unroll=4)
     yx_ref[:, :features] = dot(y_ref[0].astype(BF), back).astype(BF)
     yx_ref[:, features:] = dot(y_ref[1].astype(BF), back).astype(BF)
 
@@ -368,43 +368,52 @@
                 pl.when(a < d if side == 0 else a > d)(along(h, d, side).wait_send)
 
 
-def gather_kernel(n, in_ref, out_ref, local_sem, send_sem, recv_sem):
+def gather_kernel(n, pieces, in_ref, out_ref, local_sem, send_sem, recv_sem):
     p, i = lax.axis_index("dp"), lax.axis_index("expert")
     line = n // 2
     a, b = i // 2, i % 2
     other = a * 2 + 1 - b
     always = a >= 0
     has_left, has_right = a > 0, a < line - 1
+    rows = in_ref.shape[0] // pieces
     greet(
         [(always, p, other), (has_left, p, i - 2), (has_right, p, i + 2)],
         1 + has_left.astype(jnp.int32) + has_right.astype(jnp.int32),
     )
+    started = []
+
+    def send(condition, own, h, chunk, target):
+        at = pl.ds(h * rows, rows)
+        src = in_ref.at[at] if own else out_ref.at[chunk, at]
+        copy = remote(
+            src, out_ref.at[chunk, at], send_sem.at[len(started)], recv_sem.at[h, chunk], p, target
+        )
+        started.append((condition, copy))
+        pl.when(condition)(copy.start)
+
+    def arrive(condition, h, chunk):
+        at = pl.ds(h * rows, rows)
+        copy = remote(in_ref.at[at], out_ref.at[chunk, at], send_sem.at[0], recv_sem.at[h, chunk], p, other)
+        pl.when(condition)(copy.wait_recv)
+
+    for h in range(pieces):
+        send(has_right, True, h, i, i + 2)
+        send(has_left, True, h, i, i - 2)
+        send(always, True, h, i, other)
     own = pltpu.make_async_copy(in_ref, out_ref.at[i], local_sem)
     own.start()
-    started = []
-
-    def send(condition, src, chunk, target):
-        copy = remote(src, out_ref.at[chunk], send_sem.at[len(started)], recv_sem.at[chunk], p, target)
-        started.append((condition, copy))
-        pl.when(condition)(copy.start)
-
-    def arrive(condition, chunk):
-        copy = remote(in_ref, out_ref.at[chunk], send_sem.at[0], recv_sem.at[chunk], p, other)
-        pl.when(condition)(copy.wait_recv)
-
-    send(has_right, in_ref, i, i + 2)
-    send(has_left, in_ref, i, i - 2)
-    send(always, in_ref, i, other)
     for step in range(1, line):
-        for sign in (-1, 1):
-            from_there = (a >= step) if sign < 0 else (a + step < line)
-            further = has_right if sign < 0 else has_left
-            chunk = jnp.where(from_there, i + 2 * sign * step, i)
-            arrive(from_there, chunk)
-            send(from_there & further, out_ref.at[chunk], chunk, i - 2 * sign)
-            send(from_there, out_ref.at[chunk], chunk, other)
+        for h in range(pieces):
+            for sign in (-1, 1):
+                from_there = (a >= step) if sign < 0 else (a + step < line)
+                further = has_right if sign < 0 else has_left
+                chunk = jnp.where(from_there, i + 2 * sign * step, i)
+                arrive(from_there, h, chunk)
+                send(from_there & further, False, h, chunk, i - 2 * sign)
+                send(from_there, False, h, chunk, other)
     for k in range(line):
-        arrive(always, 2 * k + 1 - b)
+        for h in range(pieces):
+            arrive(always, h, 2 * k + 1 - b)
     for condition, copy in started:
         pl.when(condition)(copy.wait_send)
     own.wait()
@@ -498,7 +507,7 @@
     span = top * hidden
     partial_rows = partial_rows.reshape(n, local, 3 * span)
     if direct:
-        pieces = 2 if local % 32 == 0 else 1
+        pieces = 4 if local % 64 == 0 else 1
         slots = (n // 2, local, 3 * span)
         vmem = pl.BlockSpec(memory_space=pltpu.VMEM)
         mine = pl.pallas_call(
@@ -525,11 +534,11 @@
         mine = jnp.concatenate(parts, axis=1)
     if direct:
         everyone = pl.pallas_call(
-            functools.partial(gather_kernel, n),
+            functools.partial(gather_kernel, n, 2 if local % 32 == 0 else 1),
             in_specs=[ANY],
             out_specs=ANY,
             out_shape=jax.ShapeDtypeStruct((n, local, 3 * span), BF),
-            scratch_shapes=[DMA, DMA((2 * n + 8,)), DMA((n,))],
+            scratch_shapes=[DMA, DMA((4 * n + 8,)), DMA((2, n))],
             compiler_params=comm_params(1),
         )(mine).reshape(total, 3 * span)
     else:

time: 245 us -> 220 us (0.90)
  Pallas kernels: 231 us -> 207 us
    pallas_call x1, Pallas kernels: 24.7 us -> 15.6 us  [shards(): pl.pallas_call(pre_kernel, grid=(blocks,), in_specs=[rows_of((block, 2 *...]
    pallas_call x1, Pallas kernels: 33.7 us -> 24.8 us  [shards(): pl.pallas_call(post_kernel, grid=(blocks,), in_specs=[rows_of((block, 3 *...]
    pallas_call x1, Pallas kernels: 74.1 us -> 68.9 us  [shards(): pl.pallas_call(functools.partial(reduce_kernel, n, pieces), in_specs=[vme...]
where the time goes in v3:
time: 220 us
  Pallas kernels  207 us (94%)
  local copies, waits for them, and re-layouts  7.87 us (4%)
  other arithmetic  3.26 us (1%)
    pallas_call x1, Pallas kernels, shards(): pl.pallas_call(functools.partial(reduce_kernel, n, pieces), in_specs=[vme...  68.9 us
    pallas_call x1, Pallas kernels, shards(): pl.pallas_call(functools.partial(gather_kernel, n, 2 if local % 32 == 0 e...  54.1 us
    pallas_call x1, Pallas kernels, shards(): pl.pallas_call(functools.partial(scatter_kernel, n, dpn), in_specs=[ANY,...  26.1 us
    pallas_call x1, Pallas kernels, shards(): pl.pallas_call(post_kernel, grid=(blocks,), in_specs=[rows_of((block, 3 *...  24.8 us
    pallas_call x1, Pallas kernels, shards(): pl.pallas_call(functools.partial(collect_kernel, n, dpn), in_specs=[ANY],...  17.3 us
    pallas_call x1, Pallas kernels, shards(): pl.pallas_call(pre_kernel, grid=(blocks,), in_specs=[rows_of((block, 2 *...  15.6 us

profile of v3, /device:TPU:14, one launch (start us, length us, event | category | flops | bytes accessed | tf_op | source)
XLA Modules:
  0.0 219.9 jit_solution(5166531888833302106)
XLA Ops:
  0.6 0.8 slice_bitcast_fusion.5
  1.4 0.1 convert_reduce_fusion.3
  1.5 0.1 convert_reduce_fusion.2
  1.6 0.8 slice_bitcast_fusion.4
  2.4 0.7 broadcast_multiply_fusion
  3.1 0.1 mul.79
  3.2 0.7 reshape.218.want_ref
  3.8 0.1 rem.36
  3.9 0.1 rem.37
  4.0 0.7 slice_bitcast_fusion.1
  4.7 0.1 select_reduce_fusion
  4.8 0.1 copy.47
  4.9 0.1 reduce_sum.68
  5.0 0.1 copy.44
  5.1 0.1 reduce_sum.63
  5.2 0.1 copy.46
  5.2 0.1 mul.89
  5.3 0.1 copy.43
  5.4 0.1 mul.81
  5.5 0.1 fusion.3
  5.6 0.2 convert_reduce_fusion.1
  5.8 0.2 convert_reduce_fusion
  6.0 0.1 reshape.223
  6.1 0.1 copy.48
  6.2 0.1 reshape.222
  6.3 0.1 copy.45
  6.3 0.7 add_select_fusion
  7.1 0.1 select_n.59
  7.2 0.1 broadcast_in_dim.12
  7.2 0.1 reshape.224
  7.3 0.9 stack_reshape.6
  8.2 0.1 copy.39
  8.3 0.9 stack_reshape.7
  9.1 0.1 copy.40
  9.3 0.3 maximum_bitcast_fusion
  9.6 0.7 reshape.217.send_ref
  10.3 1.3 fusion.6.scale_ref
  11.6 26.1 %shard_map.128 = (bf16[8,64,512]{2,1,0:T(8,128)(2,1)}, s32[8,4,128]{2,1,0:T(4,128)}) custom-call(bf16[2,64,512]{2,1,0:T(8,128)(2,1)} %reshape.217.send_ref, s32[4,128]{1,0:T(4,128)} %reshape.218.want_ref), custom_call_target="tpu_custom_call" | custom-call | tf_op jit(solution)/shard_map/pallas_call | solution.py:468
  37.7 15.6 %shard_map.129 = bf16[512,4608]{1,0:T(8,128)(2,1)} custom-call(bf16[512,512]{1,0:T(8,128)(2,1)} %bitcast.35, s32[32,1,128]{2,1,0:T(1,128)} %bitcast.38, bf16[16,128,384]{2,1,0:T(8,128)(2,1)} %wg_ref.3, bf16[16,128,384]{2,1,0:T(8,128)(2,1)} %wu_ref.3, bf16[16,128,384]{2,1,0:T(8,128)(2,1)} %wd_ref.3), custom_call_target="tpu_custom_call" | custom-call | tf_op jit(solution)/shard_map/pallas_call | solution.py:489
  53.3 68.9 %shard_map.130.in_ref = bf16[64,4608]{1,0:T(8,128)(2,1)} custom-call(bf16[8,64,4608]{2,1,0:T(8,128)(2,1)} %bitcast.34, f32[64,1536]{1,0:T(8,128)} %fusion.6.scale_ref), custom_call_target="tpu_custom_call" | custom-call | tf_op jit(solution)/shard_map/pallas_call | solution.py:513
  122.2 54.1 %shard_map.131 = bf16[8,64,4608]{2,1,0:T(8,128)(2,1)} custom-call(bf16[64,4608]{1,0:T(8,128)(2,1)} %shard_map.130.in_ref), custom_call_target="tpu_custom_call" | custom-call | tf_op jit(solution)/shard_map/pallas_call | solution.py:536
  176.3 24.8 %shard_map.132 = (bf16[512,512]{1,0:T(8,128)(2,1)}, bf16[16,128,384]{2,1,0:T(8,128)(2,1)}, bf16[16,128,384]{2,1,0:T(8,128)(2,1)}, bf16[16,128,384]{2,1,0:T(8,128)(2,1)}) custom-call(bf16[512,4608]{1,0:T(8,128)(2,1)} %bitcast.33, bf16[512,512]{1,0:T(8,128)(2,1)} %bitcast.36, s32[32,1,128]{2,1,0:T(1,128)} %bitcast.39, bf16[16,128,384]{2,1,0:T(8,128)(2,1)} %wg_ref.3, ...), custom_call_target="tpu_custom_call" | custom-call | tf_op jit(solution)/shard_map/pallas_call | solution.py:547
  201.1 17.3 %shard_map.133 = bf16[2,64,512]{2,1,0:T(8,128)(2,1)} custom-call(bf16[8,64,512]{2,1,0:T(8,128)(2,1)} %bitcast.37), custom_call_target="tpu_custom_call" | custom-call | tf_op jit(solution)/shard_map/pallas_call | solution.py:569
  218.3 1.5 fusion.5
  (10 shorter events, 0.1 us)
